TPU v7x, 128 devices: a whole 4x4x4 slice. The times are simulated.
128 devices in a mesh: dp: 8 (over x, z_hi), stream: 16 (over y, z_lo, core).
Axes of the slice: x: 4, y: 4, z: 4 (z_hi: 2, z_lo: 2; z = z_hi * 2 + z_lo), core: 2. Of those that a mesh axis runs over, the one named last changes fastest.
Arguments:
- source_embed: bfloat16 [32768, 256], P(('dp', 'stream')), may hold values from -6 to 6
- source_labels: int32 [32768], P(('dp', 'stream')), may hold values from 0 to 63
- target_embed: bfloat16 [8192, 256], P('stream'), may hold values from -6 to 6
- target_labels: int32 [8192], P('stream'), may hold values from 0 to 63
- label_table: bfloat16 [64, 64], replicated, may hold values from 0 to 2
Outputs:
- source_potential: float32 [32768], P(('dp', 'stream'))
- target_dual: float32 [8192], P('stream')
All inputs are finite; a program needn't handle non-finite values.
Results may differ from a plain program's by a relative error of at most 0.0003.
Values may be sent and summed in bfloat16 or wider, within the bound.
A program may use at most 64 MiB of HBM per device.

v0:
```python
import functools
import math

import jax
import jax.numpy as jnp
from jax import lax
from jax.experimental import pallas as pl
from jax.experimental.pallas import tpu as pltpu
from jax.sharding import PartitionSpec as P

MESH = pl.DeviceIdType.MESH
SCALE = 0.02
LOG2E = 1.0 / math.log(2.0)
COST_TO_BITS = LOG2E / SCALE

SRC = 256
HALF = 128
TGT = 512
EMB = 256
LABELS = 64
AUX = 16
CHUNKS = 4
QUARTERS = 4
ROWS = QUARTERS * 256
COLS = 2 * CHUNKS * 256
LANES = 128
TILES = COLS // LANES
NT = (((1,), (1,)), ((), ()))


def place():
    dp, stream = lax.axis_index("dp"), lax.axis_index("stream")
    div, rem = lax.div, lax.rem
    return div(dp, 2), div(stream, 4), rem(dp, 2) * 2 + rem(div(stream, 2), 2), rem(stream, 2)


def device(x, y, z, core):
    x, y, z, core = lax.rem(x, 4), lax.rem(y, 4), lax.rem(z, 4), lax.rem(core, 2)
    return (x * 2 + lax.div(z, 2), y * 4 + lax.rem(z, 2) * 2 + core)


def split3(value):
    high = value.astype(jnp.bfloat16).astype(jnp.float32)
    rest = value - high
    middle = rest.astype(jnp.bfloat16).astype(jnp.float32)
    return high, middle, rest - middle


def aux_rows(embed, labels):
    count = embed.shape[0]
    wide = embed.astype(jnp.float32)
    square = wide * wide
    high = square.astype(jnp.bfloat16)
    low = (square - high.astype(jnp.float32)).astype(jnp.bfloat16)
    ones = jnp.ones((AUX, EMB), jnp.bfloat16)
    norm = lax.dot_general(ones, high, NT, preferred_element_type=jnp.float32)
    norm += lax.dot_general(ones, low, NT, preferred_element_type=jnp.float32)
    first, second, third = split3(norm * (-128.0 / EMB))
    row = lax.broadcasted_iota(jnp.int32, (AUX, count), 0)
    marks = jnp.broadcast_to(labels.astype(jnp.float32), (AUX, count))
    out = jnp.where(row == 0, marks, 0.0)
    out = jnp.where(row == 1, first, out)
    out = jnp.where(row == 2, second, out)
    out = jnp.where(row == 3, third, out)
    return out.astype(jnp.bfloat16)


def kernel(
    src_ref, src_labels_ref, tgt_ref, tgt_labels_ref, table_ref, f_out, g_out,
    src_labels, tgt_labels, table, src, tgt, src_side, tgt_side, block, plan, peak, col_max, weight, weight_now, partial,
    spread, s_msg, t_msg, f_first, top_dense, g_first,
    in_sem, gather_send, gather_recv, s_send, s_recv, t_send, t_recv, plane_sem,
):
    x, y, z, core = place()
    z_lo = lax.rem(z, 2)
    s_peers = [(dy, dc) for dy in (2, 1, 3, 0) for dc in range(2) if (dy, dc) != (0, 0)]
    t_peers = [(dx, dz) for dx in (2, 1, 3, 0) for dz in (2, 1, 3, 0) if (dx, dz) != (0, 0)]
    f32 = jnp.float32

    near = [device(x, y + k, z, core) for k in (1, 2, 3)] + [device(x, y, z, core + 1)]
    near += [device(x, y, z + k, core) for k in (1, 2, 3)] + [device(x + k, y, z, core) for k in (1, 2, 3)]
    barrier = pltpu.get_barrier_semaphore()
    for target in near:
        pl.semaphore_signal(barrier, inc=1, device_id=target, device_id_type=MESH)

    loads = [
        pltpu.make_async_copy(
            src_ref.at[pl.ds(h * HALF, HALF)], src.at[h, y, core, pl.ds(0, HALF)], in_sem.at[h]
        )
        for h in range(2)
    ]
    loads += [
        pltpu.make_async_copy(
            tgt_ref.at[pl.ds(h * 256, 256)], tgt.at[2 * z_lo + h, pl.ds(0, 256)], in_sem.at[2 + h]
        )
        for h in range(2)
    ]
    loads += [
        pltpu.make_async_copy(src_labels_ref, src_labels, in_sem.at[4]),
        pltpu.make_async_copy(tgt_labels_ref, tgt_labels, in_sem.at[5]),
        pltpu.make_async_copy(table_ref, table, in_sem.at[6]),
    ]
    for load in loads:
        load.start()
    loads[4].wait()
    for h in range(2):
        loads[h].wait()
        src[h, y, core, pl.ds(HALF, AUX), 0:HALF] = aux_rows(
            src[h, y, core, pl.ds(0, HALF)], src_labels[:, h * HALF : (h + 1) * HALF]
        )
    loads[5].wait()
    for h in range(2):
        loads[2 + h].wait()
        tgt[2 * z_lo + h, pl.ds(256, AUX)] = aux_rows(
            tgt[2 * z_lo + h, pl.ds(0, 256)], tgt_labels[:, h * 256 : (h + 1) * 256]
        )

    pl.semaphore_wait(barrier, len(near))

    def send(ref, k, target):
        copy = pltpu.make_async_remote_copy(
            src_ref=ref, dst_ref=ref, send_sem=gather_send.at[k], recv_sem=gather_recv.at[k],
            device_id=target, device_id_type=MESH,
        )
        copy.start()
        return copy

    def arrived(ref, k):
        pltpu.make_async_copy(ref, ref, gather_recv.at[k]).wait()

    started = []
    for h in range(2):
        own = src.at[h, y, core]
        started += [send(own, 7 * h + k, device(x, y + k, z, core)) for k in (2, 1, 3)]
        started.append(send(own, 7 * h, device(x, y, z, core + 1)))
        if h == 0:
            started += [
                send(tgt.at[2 * z_lo + q], 14 + q, device(x, y, z + 1 + 2 * q, core)) for q in range(2)
            ]
    for k in (1, 2, 3):
        pl.semaphore_signal(plane_sem, inc=1, device_id=device(x + k, y, z, core), device_id_type=MESH)

    def cols_of(piece):
        h, chunk, c = piece
        return pl.ds(pl.multiple_of(((h * CHUNKS + chunk) * 2 + c) * HALF, HALF), HALF)

    def prepare_source(pieces, slot):
        aux = [src[h, chunk, c, pl.ds(HALF, AUX), 0:HALF].astype(f32) for h, chunk, c in pieces]
        aux = jnp.concatenate(aux, axis=1)
        row = lax.broadcasted_iota(jnp.int32, (LANES, 256), 0)
        side = jnp.where(row.astype(f32) == aux[0:1], 1.0, 0.0)
        side = jnp.where((row >= 67) & (row < 70), 1.0, side)
        for k in range(3):
            side = jnp.where(row == LABELS + k, aux[1 + k : 2 + k], side)
        src_side[slot] = side.astype(jnp.bfloat16)

    def prepare_target(quarter):
        aux = tgt[quarter, pl.ds(256, AUX)].astype(f32)
        row = lax.broadcasted_iota(jnp.int32, (LABELS, 256), 0)
        onehot = jnp.where(row.astype(f32) == aux[0:1], 1.0, 0.0).astype(jnp.bfloat16)
        costs = jnp.dot(table[...], onehot, preferred_element_type=f32) * -128.0
        rest = jnp.where(row < 3, 1.0, 0.0)
        for k in range(3):
            rest = jnp.where(row == 3 + k, aux[1 + k : 2 + k], rest)
        tgt_side[quarter] = jnp.concatenate([costs, rest], axis=0).T.astype(jnp.bfloat16)

    def costs(quarter, pieces, slot):
        rows = jnp.concatenate([src[h, chunk, c, pl.ds(0, HALF)] for h, chunk, c in pieces], axis=0)
        dot = lax.dot_general(tgt[quarter, pl.ds(0, 256)], rows, NT, preferred_element_type=f32)
        dot += jnp.dot(tgt_side[quarter], src_side[slot], preferred_element_type=f32)
        dot = dot * (COST_TO_BITS / 128.0)
        top = jnp.max(dot.reshape(32, 8, 256), axis=0)
        for i, piece in enumerate(pieces):
            at = slice(i * HALF, (i + 1) * HALF)
            block[pl.ds(pl.multiple_of(quarter * 256, 256), 256), cols_of(piece)] = dot[:, at]
            peak[quarter, :, cols_of(piece)] = top[:, at]

    def first_rows(pieces):
        tops = [jnp.max(jnp.max(peak[:, :, cols_of(p)], axis=0), axis=0, keepdims=True) for p in pieces]

        def add(step, totals):
            rows = pl.ds(pl.multiple_of(step * 256, 256), 256)
            values = [jnp.exp2(block[rows, cols_of(p)] - top) for p, top in zip(pieces, tops)]
            return tuple(t + jnp.sum(v.reshape(8, 32, HALF), axis=0) for t, v in zip(totals, values))

        totals = lax.fori_loop(0, ROWS // 256, add, (jnp.zeros((32, HALF), f32),) * 2)
        for (h, chunk, c), top, total in zip(pieces, tops, totals):
            s_msg[0, h, 0, c, pl.ds(chunk, 1)] = top + jnp.log2(jnp.sum(total, axis=0, keepdims=True))

    def whole(pieces):
        slot = pieces[0][0]
        prepare_source(pieces, slot)
        for quarter in range(QUARTERS):
            costs(quarter, pieces, slot)
        first_rows(pieces)

    def chunk_at(k):
        return lax.rem(y + 4 - k, 4)

    def take(h, k):
        ref = src.at[h, chunk_at(k), core]
        arrived(ref, 7 * h + k)
        started.append(send(ref, 7 * h + 3 + k, device(x, y, z, core + 1)))

    def exchange_s(turn, h):
        for dy, dc in s_peers:
            pltpu.make_async_remote_copy(
                src_ref=s_msg.at[turn, h, 0], dst_ref=s_msg.at[turn, h, dy * 2 + dc],
                send_sem=s_send.at[turn, h], recv_sem=s_recv.at[turn, h],
                device_id=device(x, y + dy, z, core + dc), device_id_type=MESH,
            ).start()

    def exchanged_s(turn, h):
        others = s_msg.at[turn, h, pl.ds(1, 7)]
        pltpu.make_async_copy(others, others, s_recv.at[turn, h]).wait()

    def exchange_t(turn):
        for dx, dz in t_peers:
            pltpu.make_async_remote_copy(
                src_ref=t_msg.at[turn, 0], dst_ref=t_msg.at[turn, dx * 4 + dz],
                send_sem=t_send.at[turn], recv_sem=t_recv.at[turn],
                device_id=device(x + dx, y, z + dz, core), device_id_type=MESH,
            ).start()
        others = t_msg.at[turn, pl.ds(1, 15)]
        pltpu.make_async_copy(others, others, t_recv.at[turn]).wait()

    away = 2 * (1 - z_lo)
    own = [[(h, y, c) for c in range(2)] for h in range(2)]
    loads[6].wait()
    for quarter in range(2):
        prepare_target(2 * z_lo + quarter)
    for h in range(2):
        arrived(src.at[h, y, 1 - core], 7 * h)
        prepare_source(own[h], h)
        for quarter in range(2):
            costs(2 * z_lo + quarter, own[h], h)
    for quarter in range(2):
        arrived(tgt.at[away + quarter], 14 + quarter)
        prepare_target(away + quarter)
        for h in range(2):
            costs(away + quarter, own[h], h)
    for h in range(2):
        first_rows(own[h])
    for h in range(2):
        for k in (1, 3, 2):
            take(h, k)
        whole([(h, chunk_at(1), core), (h, chunk_at(3), core)])
        other = 1 - core
        arrived(src.at[h, chunk_at(1), other], 7 * h + 4)
        whole([(h, chunk_at(2), core), (h, chunk_at(1), other)])
        arrived(src.at[h, chunk_at(3), other], 7 * h + 6)
        arrived(src.at[h, chunk_at(2), other], 7 * h + 5)
        whole([(h, chunk_at(3), other), (h, chunk_at(2), other)])
        exchange_s(0, h)

    source_count = COLS * 16.0
    target_count = ROWS * 8.0

    def joined(parts):
        top = jnp.max(parts, axis=0)
        return top + jnp.log2(jnp.sum(jnp.exp2(parts - top), axis=0))

    def spread_rows(h, values):
        for i in range(2 * CHUNKS):
            spread[:, tile(h * 2 * CHUNKS + i)] = jnp.broadcast_to(values[i % 2, i // 2 : i // 2 + 1], (8, HALF))

    def tile(l):
        return slice(l * LANES, (l + 1) * LANES)

    def tiles_of(h):
        return range(h * TILES // 2, (h + 1) * TILES // 2)

    def as_columns(values, b):
        return jnp.broadcast_to(values[b : b + 1], (LANES, LANES)).T

    def lane_reduced(op, ref, b):
        return op(ref[tile(b), :].T, axis=0, keepdims=True)

    def by_rows(step, count=8):
        return [pl.ds(pl.multiple_of((step * count + s) * 8, 8), 8) for s in range(count)]

    def first_columns(h):
        across = [spread[:, tile(l)] for l in tiles_of(h)]

        def find(step, _):
            for rows in by_rows(step):
                top = None
                for l, given in zip(tiles_of(h), across):
                    value = block[rows, tile(l)] + given
                    top = value if top is None else jnp.maximum(top, value)
                partial[h, rows, :] = top
            return 0

        lax.fori_loop(0, ROWS // 64, find, 0)
        for b in range(8):
            top = lane_reduced(jnp.max, partial.at[h], b)
            top_dense[h, b : b + 1] = top
            col_max[h, tile(b), :] = jnp.broadcast_to(top, (LANES, LANES)).T

        def add(step, _):
            for rows in by_rows(step):
                top, total = col_max[h, rows, :], None
                for l, given in zip(tiles_of(h), across):
                    value = jnp.exp2(block[rows, tile(l)] + (given - top))
                    plan[rows, tile(l)] = value
                    total = value if total is None else total + value
                partial[h, rows, :] = total
            return 0

        lax.fori_loop(0, ROWS // 64, add, 0)
        sums = [lane_reduced(jnp.sum, partial.at[h], b) for b in range(8)]
        return top_dense[h] + jnp.log2(jnp.concatenate(sums, axis=0))

    logs = []
    for h in range(2):
        exchanged_s(0, h)
        f_now = math.log2(target_count) - joined(s_msg[0, h])
        f_first[h] = f_now
        spread_rows(h, f_now)
        logs.append(first_columns(h))
    top = jnp.maximum(logs[0], logs[1])
    t_msg[0, 0] = top + jnp.log2(jnp.exp2(logs[0] - top) + jnp.exp2(logs[1] - top))
    pl.semaphore_wait(plane_sem, 3)
    exchange_t(0)
    g_now = math.log2(source_count) - joined(t_msg[0])
    g_first[...] = g_now
    for h in range(2):
        scale = jnp.exp2(top_dense[h] + g_now)
        for b in range(8):
            weight[h, tile(b), :] = as_columns(scale, b)

    def row_sums(turn, h):
        def add(step, totals):
            for rows in by_rows(step):
                w = (weight if turn == 1 else weight_now)[h, rows, :]
                totals = tuple(total + plan[rows, tile(l)] * w for total, l in zip(totals, tiles_of(h)))
            return totals

        totals = lax.fori_loop(0, ROWS // 64, add, tuple(jnp.zeros((8, LANES), f32) for _ in tiles_of(h)))
        for i, total in enumerate(totals):
            s_msg[turn, h, 0, i % 2, i // 2 : i // 2 + 1] = jnp.sum(total, axis=0, keepdims=True)

    def column_sums(h):
        across = [spread[:, tile(l)] for l in tiles_of(h)]

        def add(step, _):
            for rows in by_rows(step):
                total = None
                for l, given in zip(tiles_of(h), across):
                    value = plan[rows, tile(l)] * given
                    total = value if total is None else total + value
                total = total * weight[h, rows, :]
                partial[0, rows, :] = total if h == 0 else total + partial[0, rows, :]
            return 0

        lax.fori_loop(0, ROWS // 64, add, 0)

    for turn in (1, 2):
        for h in range(2):
            row_sums(turn, h)
            exchange_s(turn, h)
        for h in range(2):
            exchanged_s(turn, h)
            u_now = target_count / jnp.sum(s_msg[turn, h], axis=0)
            spread_rows(h, u_now)
            column_sums(h)
            if turn == 2:
                f_first[h] = (f_first[h] + jnp.log2(u_now)) * (1.0 / COST_TO_BITS)
        for b in range(8):
            t_msg[turn, 0, b : b + 1] = lane_reduced(jnp.sum, partial.at[0], b)
        exchange_t(turn)
        v_now = source_count / jnp.sum(t_msg[turn], axis=0)
        if turn == 1:
            for b in range(8):
                column = as_columns(v_now, b)
                for h in range(2):
                    weight_now[h, tile(b), :] = weight[h, tile(b), :] * column

    for h in range(2):
        f_out[h : h + 1] = f_first[h, core, pl.ds(y, 1)]
    g_first[...] = (g_first[...] + jnp.log2(v_now)) * (1.0 / COST_TO_BITS)
    g_out[...] = g_first[pl.ds(z_lo * 4, 4)]

    for copy in started:
        copy.wait_send()
    for turn in range(3):
        for h in range(2):
            others = s_msg.at[turn, h, pl.ds(1, 7)]
            pltpu.make_async_copy(others, others, s_send.at[turn, h]).wait()
        others = t_msg.at[turn, pl.ds(1, 15)]
        pltpu.make_async_copy(others, others, t_send.at[turn]).wait()


def hand_on(f_ref, g_ref, f_out, g_out):
    f_out[...] = f_ref[...]
    g_out[...] = g_ref[...]


def body(source_embed, source_labels, target_embed, target_labels, label_table):
    vmem, hbm = pl.BlockSpec(memory_space=pltpu.VMEM), pl.BlockSpec(memory_space=pltpu.HBM)
    f32, bf16, dma = jnp.float32, jnp.bfloat16, pltpu.SemaphoreType.DMA
    f, g = pl.pallas_call(
        kernel,
        out_shape=(jax.ShapeDtypeStruct((2, HALF), f32), jax.ShapeDtypeStruct((4, LANES), f32)),
        in_specs=[hbm] * 5,
        out_specs=(vmem, vmem),
        scratch_shapes=[
            pltpu.VMEM((1, SRC), jnp.int32),
            pltpu.VMEM((1, TGT), jnp.int32),
            pltpu.VMEM((LABELS, LABELS), bf16),
            pltpu.VMEM((2, CHUNKS, 2, HALF + AUX, EMB), bf16),
            pltpu.VMEM((QUARTERS, 256 + AUX, EMB), bf16),
            pltpu.VMEM((2, LANES, 256), bf16),
            pltpu.VMEM((QUARTERS, 256, LANES), bf16),
            pltpu.VMEM((ROWS, COLS), f32),
            pltpu.VMEM((ROWS, COLS), f32),
            pltpu.VMEM((QUARTERS, 8, COLS), f32),
            pltpu.VMEM((2, ROWS, LANES), f32),
            pltpu.VMEM((2, ROWS, LANES), f32),
            pltpu.VMEM((2, ROWS, LANES), f32),
            pltpu.VMEM((2, ROWS, LANES), f32),
            pltpu.VMEM((8, COLS), f32),
            pltpu.VMEM((3, 2, 8, 2, CHUNKS, LANES), f32),
            pltpu.VMEM((3, 16, 8, LANES), f32),
            pltpu.VMEM((2, 2, CHUNKS, LANES), f32),
            pltpu.VMEM((2, 8, LANES), f32),
            pltpu.VMEM((8, LANES), f32),
            dma((7,)),
            dma((16,)),
            dma((16,)),
            dma((3, 2)),
            dma((3, 2)),
            dma((3,)),
            dma((3,)),
            pltpu.SemaphoreType.REGULAR,
        ],
        compiler_params=pltpu.CompilerParams(collective_id=0, has_side_effects=True, vmem_limit_bytes=60 << 20),
    )(
        source_embed,
        source_labels.reshape(1, SRC),
        target_embed,
        target_labels.reshape(1, TGT),
        label_table,
    )
    f, g = pl.pallas_call(
        hand_on,
        out_shape=(jax.ShapeDtypeStruct((2, HALF), f32), jax.ShapeDtypeStruct((4, LANES), f32)),
        in_specs=[vmem] * 2,
        out_specs=(vmem, vmem),
    )(f, g)
    return f.reshape(SRC), g.reshape(TGT)


def solution(mesh):
    placed = (P(("dp", "stream"), None), P(("dp", "stream")), P("stream", None), P("stream"), P())
    return jax.shard_map(
        body,
        mesh=mesh,
        in_specs=placed,
        out_specs=(P(("dp", "stream")), P("stream")),
        check_vma=False,
    )
```

profile of v0, /device:TPU:1, one launch (start us, length us, event | category | flops | bytes accessed | tf_op | source)
XLA Modules:
  0.0 51.2 jit_solution(18384665930362342298)
XLA Ops:
  0.6 49.3 %shard_map.68 = (f32[2,128]{1,0:T(2,128)}, f32[4,128]{1,0:T(4,128)}) custom-call(bf16[256,256]{1,0:T(8,128)(2,1)} %src_ref.1, s32[1,256]{1,0:T(1,128)} %bitcast.5, bf16[512,256]{1,0:T(8,128)(2,1)} %tgt_ref.1, s32[1,512]{1,0:T(1,128)} %bitcast.4, bf16[64,64]{1,0:T(8,128)(2,1)} %table_ref.1), custom_call_target="tpu_custom_call" | custom-call | tf_op jit(solution)/shard_map/pallas_call | solution.py:402
  50.0 1.3 %shard_map.69 = (f32[2,128]{1,0:T(2,128)}, f32[4,128]{1,0:T(4,128)}) custom-call(f32[2,128]{1,0:T(2,128)} %get-tuple-element.6.f_ref, f32[4,128]{1,0:T(4,128)} %get-tuple-element.7.g_ref), custom_call_target="tpu_custom_call" | custom-call | tf_op jit(solution)/shard_map/pallas_call | solution.py:445
where the time goes:
time: 51.4 us; the launch traced here: 51.2 us
  Pallas kernels  50.6 us (98%)
  between operations  0.64 us (1%)
    pallas_call x1, Pallas kernels, body(): pl.pallas_call(kernel, out_shape=(jax.ShapeDtypeStruct((2, HALF), f32), j...  49.3 us
    pallas_call x1, Pallas kernels, body(): pl.pallas_call(hand_on, out_shape=(jax.ShapeDtypeStruct((2, HALF), f32),...  1.25 us

commit v1 on v0

--- a/solution.py
+++ b/solution.py
@@ -67,7 +67,7 @@
 
 def kernel(
     src_ref, src_labels_ref, tgt_ref, tgt_labels_ref, table_ref, f_out, g_out,
-    src_labels, tgt_labels, table, src, tgt, src_side, tgt_side, block, plan, peak, col_max, weight, weight_now, partial,
+    src_labels, tgt_labels, table, src, tgt, src_side, tgt_side, block, plan, peak, col_max, weight, partial,
     spread, s_msg, t_msg, f_first, top_dense, g_first,
     in_sem, gather_send, gather_recv, s_send, s_recv, t_send, t_recv, plane_sem,
 ):
@@ -214,13 +214,15 @@
         others = s_msg.at[turn, h, pl.ds(1, 7)]
         pltpu.make_async_copy(others, others, s_recv.at[turn, h]).wait()
 
-    def exchange_t(turn):
+    def send_t(turn):
         for dx, dz in t_peers:
             pltpu.make_async_remote_copy(
                 src_ref=t_msg.at[turn, 0], dst_ref=t_msg.at[turn, dx * 4 + dz],
                 send_sem=t_send.at[turn], recv_sem=t_recv.at[turn],
                 device_id=device(x + dx, y, z + dz, core), device_id_type=MESH,
             ).start()
+
+    def received_t(turn):
         others = t_msg.at[turn, pl.ds(1, 15)]
         pltpu.make_async_copy(others, others, t_recv.at[turn]).wait()
 
@@ -273,43 +275,37 @@
     def as_columns(values, b):
         return jnp.broadcast_to(values[b : b + 1], (LANES, LANES)).T
 
-    def lane_reduced(op, ref, b):
-        return op(ref[tile(b), :].T, axis=0, keepdims=True)
-
-    def by_rows(step, count=8):
-        return [pl.ds(pl.multiple_of((step * count + s) * 8, 8), 8) for s in range(count)]
+    def rows_in(b):
+        return [slice(b * LANES + i * 8, b * LANES + i * 8 + 8) for i in range(LANES // 8)]
+
+    def lane_reduced(op, tiles):
+        return op(jnp.concatenate(tiles, axis=0).T, axis=0, keepdims=True)
 
     def first_columns(h):
         across = [spread[:, tile(l)] for l in tiles_of(h)]
-
-        def find(step, _):
-            for rows in by_rows(step):
+        logs = []
+        for b in range(8):
+            tops = []
+            for rows in rows_in(b):
                 top = None
                 for l, given in zip(tiles_of(h), across):
                     value = block[rows, tile(l)] + given
                     top = value if top is None else jnp.maximum(top, value)
-                partial[h, rows, :] = top
-            return 0
-
-        lax.fori_loop(0, ROWS // 64, find, 0)
-        for b in range(8):
-            top = lane_reduced(jnp.max, partial.at[h], b)
+                tops.append(top)
+            top = lane_reduced(jnp.max, tops)
             top_dense[h, b : b + 1] = top
             col_max[h, tile(b), :] = jnp.broadcast_to(top, (LANES, LANES)).T
-
-        def add(step, _):
-            for rows in by_rows(step):
-                top, total = col_max[h, rows, :], None
+        for b in range(8):
+            totals = []
+            for rows in rows_in(b):
+                top_column, total = col_max[h, rows, :], None
                 for l, given in zip(tiles_of(h), across):
-                    value = jnp.exp2(block[rows, tile(l)] + (given - top))
+                    value = jnp.exp2(block[rows, tile(l)] + (given - top_column))
                     plan[rows, tile(l)] = value
                     total = value if total is None else total + value
-                partial[h, rows, :] = total
-            return 0
-
-        lax.fori_loop(0, ROWS // 64, add, 0)
-        sums = [lane_reduced(jnp.sum, partial.at[h], b) for b in range(8)]
-        return top_dense[h] + jnp.log2(jnp.concatenate(sums, axis=0))
+                totals.append(total)
+            logs.append(jnp.log2(lane_reduced(jnp.sum, totals)))
+        return top_dense[h] + jnp.concatenate(logs, axis=0)
 
     logs = []
     for h in range(2):
@@ -321,60 +317,70 @@
     top = jnp.maximum(logs[0], logs[1])
     t_msg[0, 0] = top + jnp.log2(jnp.exp2(logs[0] - top) + jnp.exp2(logs[1] - top))
     pl.semaphore_wait(plane_sem, 3)
-    exchange_t(0)
+    send_t(0)
+
+    def rescale(step, _):
+        for s in range(8):
+            rows = pl.ds(pl.multiple_of(step * 64 + s * 8, 8), 8)
+            both = jnp.maximum(col_max[0, rows, :], col_max[1, rows, :])
+            for h in range(2):
+                down = jnp.exp2(col_max[h, rows, :] - both)
+                for l in tiles_of(h):
+                    block[rows, tile(l)] = plan[rows, tile(l)] * down
+        return 0
+
+    lax.fori_loop(0, ROWS // 64, rescale, 0)
+    top = jnp.maximum(top_dense[0], top_dense[1])
+    received_t(0)
     g_now = math.log2(source_count) - joined(t_msg[0])
     g_first[...] = g_now
-    for h in range(2):
-        scale = jnp.exp2(top_dense[h] + g_now)
+    scale = jnp.exp2(top + g_now)
+    def row_sums(turn, h, factors):
+        totals = [None for _ in tiles_of(h)]
         for b in range(8):
-            weight[h, tile(b), :] = as_columns(scale, b)
-
-    def row_sums(turn, h):
-        def add(step, totals):
-            for rows in by_rows(step):
-                w = (weight if turn == 1 else weight_now)[h, rows, :]
-                totals = tuple(total + plan[rows, tile(l)] * w for total, l in zip(totals, tiles_of(h)))
-            return totals
-
-        totals = lax.fori_loop(0, ROWS // 64, add, tuple(jnp.zeros((8, LANES), f32) for _ in tiles_of(h)))
+            if h == 0:
+                weight[tile(b), :] = as_columns(factors, b)
+            for rows in rows_in(b):
+                w = weight[rows, :]
+                values = [block[rows, tile(l)] * w for l in tiles_of(h)]
+                totals = [v if t is None else t + v for t, v in zip(totals, values)]
         for i, total in enumerate(totals):
             s_msg[turn, h, 0, i % 2, i // 2 : i // 2 + 1] = jnp.sum(total, axis=0, keepdims=True)
 
-    def column_sums(h):
-        across = [spread[:, tile(l)] for l in tiles_of(h)]
-
-        def add(step, _):
-            for rows in by_rows(step):
-                total = None
-                for l, given in zip(tiles_of(h), across):
-                    value = plan[rows, tile(l)] * given
-                    total = value if total is None else total + value
-                total = total * weight[h, rows, :]
-                partial[0, rows, :] = total if h == 0 else total + partial[0, rows, :]
-            return 0
-
-        lax.fori_loop(0, ROWS // 64, add, 0)
-
+    def column_sums(h, b, across):
+        totals = []
+        for rows in rows_in(b):
+            total = None if h == 0 else partial[rows, :]
+            for l, given in zip(tiles_of(h), across):
+                value = block[rows, tile(l)] * given
+                total = value if total is None else total + value
+            if h == 0:
+                partial[rows, :] = total
+            totals.append(total)
+        return totals
+
+    factors = scale
     for turn in (1, 2):
         for h in range(2):
-            row_sums(turn, h)
+            row_sums(turn, h, factors)
             exchange_s(turn, h)
+        sums = []
         for h in range(2):
             exchanged_s(turn, h)
             u_now = target_count / jnp.sum(s_msg[turn, h], axis=0)
             spread_rows(h, u_now)
-            column_sums(h)
+            across = [spread[:, tile(l)] for l in tiles_of(h)]
+            for b in range(8):
+                totals = column_sums(h, b, across)
+                if h == 1:
+                    sums.append(lane_reduced(jnp.sum, totals))
             if turn == 2:
                 f_first[h] = (f_first[h] + jnp.log2(u_now)) * (1.0 / COST_TO_BITS)
-        for b in range(8):
-            t_msg[turn, 0, b : b + 1] = lane_reduced(jnp.sum, partial.at[0], b)
-        exchange_t(turn)
+        t_msg[turn, 0] = scale * jnp.concatenate(sums, axis=0)
+        send_t(turn)
+        received_t(turn)
         v_now = source_count / jnp.sum(t_msg[turn], axis=0)
-        if turn == 1:
-            for b in range(8):
-                column = as_columns(v_now, b)
-                for h in range(2):
-                    weight_now[h, tile(b), :] = weight[h, tile(b), :] * column
+        factors = scale * v_now
 
     for h in range(2):
         f_out[h : h + 1] = f_first[h, core, pl.ds(y, 1)]
@@ -416,9 +422,8 @@
             pltpu.VMEM((ROWS, COLS), f32),
             pltpu.VMEM((QUARTERS, 8, COLS), f32),
             pltpu.VMEM((2, ROWS, LANES), f32),
-            pltpu.VMEM((2, ROWS, LANES), f32),
-            pltpu.VMEM((2, ROWS, LANES), f32),
-            pltpu.VMEM((2, ROWS, LANES), f32),
+            pltpu.VMEM((ROWS, LANES), f32),
+            pltpu.VMEM((ROWS, LANES), f32),
             pltpu.VMEM((8, COLS), f32),
             pltpu.VMEM((3, 2, 8, 2, CHUNKS, LANES), f32),
             pltpu.VMEM((3, 16, 8, LANES), f32),

time: 51.4 us -> 49.1 us (0.955)
  Pallas kernels: 50.6 us -> 48.3 us
    pallas_call x1, Pallas kernels: 49.3 us -> 47 us  [body(): pl.pallas_call(kernel, out_shape=(jax.ShapeDtypeStruct((2, HALF), f32), j...]
where the time goes in v1:
time: 49.1 us; the launch traced here: 48.9 us
  Pallas kernels  48.3 us (98%)
  between operations  0.64 us (1%)
    pallas_call x1, Pallas kernels, body(): pl.pallas_call(kernel, out_shape=(jax.ShapeDtypeStruct((2, HALF), f32), j...  47 us
    pallas_call x1, Pallas kernels, body(): pl.pallas_call(hand_on, out_shape=(jax.ShapeDtypeStruct((2, HALF), f32),...  1.25 us

profile of v1, /device:TPU:1, one launch (start us, length us, event | category | flops | bytes accessed | tf_op | source)
XLA Modules:
  0.0 48.9 jit_solution(13312461891401772583)
XLA Ops:
  0.6 47.0 %shard_map.68 = (f32[2,128]{1,0:T(2,128)}, f32[4,128]{1,0:T(4,128)}) custom-call(bf16[256,256]{1,0:T(8,128)(2,1)} %src_ref.1, s32[1,256]{1,0:T(1,128)} %bitcast.5, bf16[512,256]{1,0:T(8,128)(2,1)} %tgt_ref.1, s32[1,512]{1,0:T(1,128)} %bitcast.4, bf16[64,64]{1,0:T(8,128)(2,1)} %table_ref.1), custom_call_target="tpu_custom_call" | custom-call | tf_op jit(solution)/shard_map/pallas_call | solution.py:408
  47.7 1.3 %shard_map.69 = (f32[2,128]{1,0:T(2,128)}, f32[4,128]{1,0:T(4,128)}) custom-call(f32[2,128]{1,0:T(2,128)} %get-tuple-element.6.f_ref, f32[4,128]{1,0:T(4,128)} %get-tuple-element.7.g_ref), custom_call_target="tpu_custom_call" | custom-call | tf_op jit(solution)/shard_map/pallas_call | solution.py:450
